TPU v7x, 32 devices: a whole 2x2x4 slice. The times are simulated.
32 devices in a mesh: pop: 8 (over z, x), tensor: 4 (over y, core).
Axes of the slice: x: 2, y: 2, z: 4, core: 2. Of those that a mesh axis runs over, the one named last changes fastest.
Arguments:
- token_ids: int32 [64, 64], P('pop'), may hold values from 0 to 76031, as said below
- ranks: int32 [64], P('pop'), may hold values from 0 to 63, each once
- embed_table: bfloat16 [76032, 3584], P('pop', 'tensor'), may hold values from -6 to 6
- norm_gain: bfloat16 [3584], replicated, may hold values from 0.5 to 1.5
- gate_weight: bfloat16 [3584, 18944], P('pop', 'tensor'), may hold values from -0.09375 to 0.09375
- up_weight: bfloat16 [3584, 18944], P('pop', 'tensor'), may hold values from -0.09375 to 0.09375
- gate_left: bfloat16 [64, 3584], P('pop'), may hold values from -6 to 6
- up_left: bfloat16 [64, 3584], P('pop'), may hold values from -6 to 6
- gate_right: bfloat16 [64, 18944], P('pop', 'tensor'), may hold values from -6 to 6
- up_right: bfloat16 [64, 18944], P('pop', 'tensor'), may hold values from -6 to 6
Outputs:
- hidden: bfloat16 [4096, 18944], P('pop', 'tensor')
- gate_step: float32 [3584, 18944], P('pop', 'tensor')
- up_step: float32 [3584, 18944], P('pop', 'tensor')
Inputs may be any that keep to these rules, and one draw needn't show every extreme that they name: Split token_ids into aligned blocks of 8 members (the members of one index of pop) and the table into blocks of 9504 rows: in every block of members, at most 128 ids fall in any one block of table rows, and exactly 128 in one of them.
All inputs are finite; a program needn't handle non-finite values.
Results may differ from a plain program's by a relative error of at most 0.0058.
Values may be sent and summed in bfloat16 or wider, within the bound.
A program may use at most 256 MiB of HBM per device.

v0:
```python
import math
import jax
import jax.numpy as jnp
from jax import lax
from jax.sharding import PartitionSpec as P


def split_high(x):
    high = lax.reduce_precision(x, exponent_bits=8, mantissa_bits=7)
    low = x - high
    return jnp.concatenate([high.astype(jnp.bfloat16), low.astype(jnp.bfloat16)], axis=0)


def weighted_step(left, right, score):
    scaled = split_high(left.astype(jnp.float32) * score[:, None])
    both = jnp.concatenate([right, right], axis=0)
    return lax.dot_general(
        scaled, both, (((0,), (0,)), ((), ())), preferred_element_type=jnp.float32
    )


def per_device(
    token_ids,
    ranks,
    embed_table,
    norm_gain,
    gate_weight,
    up_weight,
    gate_left,
    up_left,
    gate_right,
    up_right,
):
    pops = lax.axis_size("pop")
    pop = lax.axis_index("pop")
    tensor = lax.axis_index("tensor")
    table_rows, features = embed_table.shape
    own_members, prompt = token_ids.shape
    row_count, hidden_cols = gate_weight.shape
    width = norm_gain.shape[0]
    members = own_members * pops
    part = -(-hidden_cols // (128 * pops)) * 128
    padded = part * pops

    def pad_cols(x):
        return jnp.pad(x, ((0, 0), (0, padded - hidden_cols)))

    all_ids = lax.all_gather(token_ids, "pop", axis=0, tiled=True)
    all_ranks = lax.all_gather(ranks, "pop", axis=0, tiled=True)
    local_ids = all_ids.reshape(-1) - pop * table_rows
    owned = (local_ids >= 0) & (local_ids < table_rows)
    picked = jnp.take(embed_table, jnp.clip(local_ids, 0, table_rows - 1), axis=0)
    partial_rows = jnp.where(owned[:, None], picked, jnp.bfloat16(0))
    own_cols = lax.psum_scatter(partial_rows, "pop", scatter_dimension=0, tiled=True)
    gate_cols = lax.all_to_all(pad_cols(gate_weight), "pop", 1, 0, tiled=True)
    up_cols = lax.all_to_all(pad_cols(up_weight), "pop", 1, 0, tiled=True)
    values = own_cols.astype(jnp.float32)
    total = lax.psum(jnp.sum(values * values, axis=-1), "tensor")
    gain = lax.dynamic_slice_in_dim(norm_gain, tensor * features, features, 0)
    own_normed = (
        values * lax.rsqrt(total[:, None] * (1.0 / width) + 1e-06) * gain.astype(jnp.float32)
    ).astype(jnp.bfloat16)
    some = lax.all_gather(own_normed, "pop", axis=0, tiled=True)
    normed = lax.all_gather(some, "tensor", axis=1, tiled=True)
    all_gl, all_ul, all_gr, all_ur = (
        lax.all_gather(gate_left, "pop", axis=0, tiled=True),
        lax.all_gather(up_left, "pop", axis=0, tiled=True),
        lax.all_gather(gate_right, "pop", axis=0, tiled=True),
        lax.all_gather(up_right, "pop", axis=0, tiled=True),
    )
    scale = 0.5 / math.sqrt(width)
    blocks = normed.reshape(members, prompt, width)

    def project(weight, left, right):
        base = jnp.dot(normed, weight, preferred_element_type=jnp.float32)
        side = jnp.einsum("mld,md->ml", blocks, left, preferred_element_type=jnp.float32) * scale
        cols = lax.dynamic_slice_in_dim(pad_cols(right), pop * part, part, 1)
        return (
            base.reshape(members, prompt, part)
            + side[:, :, None] * cols.astype(jnp.float32)[:, None, :]
        )

    gate = project(gate_cols, all_gl, all_gr)
    up = project(up_cols, all_ul, all_ur)
    mine = (jax.nn.silu(gate) * up).astype(jnp.bfloat16).reshape(members * prompt, part)
    hidden = lax.all_to_all(mine, "pop", 0, 1, tiled=True)[:, :hidden_cols]
    score = (2.0 * all_ranks.astype(jnp.float32) - (members - 1)) / (members - 1)
    score = score * (1.0 / math.sqrt(members))
    row_start = pop * row_count
    left_gate = lax.dynamic_slice_in_dim(all_gl, row_start, row_count, 1)
    left_up = lax.dynamic_slice_in_dim(all_ul, row_start, row_count, 1)
    gate_step = weighted_step(left_gate, all_gr, score)
    up_step = weighted_step(left_up, all_ur, score)
    return (hidden, gate_step, up_step)


def solution(mesh):
    in_specs = (
        P("pop", None),
        P("pop"),
        P("pop", "tensor"),
        P(),
        P("pop", "tensor"),
        P("pop", "tensor"),
        P("pop", None),
        P("pop", None),
        P("pop", "tensor"),
        P("pop", "tensor"),
    )
    out_specs = (P("pop", "tensor"), P("pop", "tensor"), P("pop", "tensor"))
    return jax.shard_map(
        per_device, mesh=mesh, in_specs=in_specs, out_specs=out_specs, check_vma=False
    )
```

profile of v0, /device:TPU:0, one launch (start us, length us, event | category | flops | bytes accessed | tf_op | source)
XLA Modules:
  0.0 799.4 jit_solution(13260142982139188664)
XLA Ops:
  7.2 0.0 reduce-scatter.2.cloned.1.call-start
  7.2 32.3 %all_gather.24 = s32[64,64]{1,0:T(8,128)S(1)} all-gather(s32[8,64]{1,0:T(8,128)} %param.10), channel_id=1, replica_groups=mesh['pop'=8,'tensor'=4] {'pop'}, dimensions={0}, use_global_device_ids=true | all-gather | bytes 18432 | tf_op jit(solution)/shard_map/all_gather | solution.py:48
  39.6 0.1 min.18
  39.7 0.1 min.16
  39.7 0.1 and.20
  39.9 27.8 %gather_fusion = bf16[4096,896]{1,0:T(8,128)(2,1)} fusion(bf16[9504,896]{1,0:T(8,128)(2,1)} %param.12, s32[4096]{0:T(1024)S(1)} %broadcast_clamp_fusion), kind=kCustom, calls=%fused_computation | custom fusion | bytes 14696448 | tf_op jit(solution)/shard_map/jit(_take)/gather | solution.py:52
  67.7 7.0 select_select_fusion
  74.7 0.0 reduce-scatter.2.cloned.1.call-update
  74.7 0.0 all-gather.3.cloned.1.call-start
  74.8 0.8 dynamic-slice_convert_fusion
  75.5 132.9 %reduce-scatter.2.cloned.1.call-done = bf16[512,896]{1,0:T(8,128)(2,1)} async-done(((bf16[4096,896]{1,0:T(8,128)(2,1)}), bf16[512,896]{1,0:T(8,128)(2,1)}) %reduce-scatter.2.cloned.1.call-update) | async-done | bytes 917520 | tf_op jit(solution)/shard_map/reduce_scatter | solution.py:54
  208.5 1.4 fusion
  209.9 5.7 psum.7
  215.6 2.4 fusion.2
  217.9 0.0 all-gather.3.cloned.1.call-update
  218.0 0.0 all-gather.5.cloned.1.call-start
  218.0 111.5 %all-gather.3.cloned.1.call-done = bf16[4096,896]{1,0:T(8,128)(2,1)} async-done(((bf16[512,896]{1,0:T(8,128)(2,1)}), bf16[4096,896]{1,0:T(8,128)(2,1)}) %all-gather.3.cloned.1.call-update) | async-done | bytes 7340048 | tf_op jit(solution)/shard_map/all_gather | solution.py:63
  329.5 0.0 all-gather.5.cloned.1.call-update
  329.5 2.8 pad.14
  332.3 2.6 copy.30
  334.9 4.8 all-to-all-start
  339.7 0.0 copy-start
  339.7 4.0 pad.16
  343.7 0.0 copy-start.1
  343.7 0.0 copy-start.2
  343.7 0.0 copy-start.3
  343.7 3.2 copy.29
  346.9 115.7 %all_gather.28 = bf16[64,4736]{1,0:T(8,128)(2,1)S(1)} all-gather(bf16[8,4736]{1,0:T(8,128)(2,1)S(1)} %copy-done), channel_id=1, replica_groups=mesh['pop'=8,'tensor'=4] {'pop'}, dimensions={0}, use_global_device_ids=true | all-gather | bytes 681984 | tf_op jit(solution)/shard_map/all_gather | solution.py:68
  462.7 31.8 %all_gather.30 = bf16[64,4736]{1,0:T(8,128)(2,1)S(1)} all-gather(bf16[8,4736]{1,0:T(8,128)(2,1)S(1)} %copy-done.1), channel_id=1, replica_groups=mesh['pop'=8,'tensor'=4] {'pop'}, dimensions={0}, use_global_device_ids=true | all-gather | bytes 681984 | tf_op jit(solution)/shard_map/all_gather | solution.py:69
  494.5 31.3 %all_gather.27 = bf16[64,3584]{1,0:T(8,128)(2,1)S(1)} all-gather(bf16[8,3584]{1,0:T(8,128)(2,1)S(1)} %copy-done.2), channel_id=1, replica_groups=mesh['pop'=8,'tensor'=4] {'pop'}, dimensions={0}, use_global_device_ids=true | all-gather | bytes 516096 | tf_op jit(solution)/shard_map/all_gather | solution.py:66
  525.8 40.9 %all_gather.29 = bf16[64,3584]{1,0:T(8,128)(2,1)S(1)} all-gather(bf16[8,3584]{1,0:T(8,128)(2,1)S(1)} %copy-done.3), channel_id=1, replica_groups=mesh['pop'=8,'tensor'=4] {'pop'}, dimensions={0}, use_global_device_ids=true | all-gather | bytes 516096 | tf_op jit(solution)/shard_map/all_gather | solution.py:67
  566.7 0.0 all-to-all-done
  566.7 15.6 %all-to-all-start.1 = ((bf16[448,8,640]{2,0,1:T(8,128)(2,1)}), bf16[448,8,640]{2,0,1:T(8,128)(2,1)}, u32[]{:S(2)}, u32[]{:S(2)}) async-start(bf16[448,8,640]{2,0,1:T(8,128)(2,1)} %bitcast.38), calls=%async_computation.2 | async-start | bytes 9175040 | tf_op jit(solution)/shard_map/all_to_all | solution.py:56
  582.3 0.0 all-gather.5.cloned.1.call-done
  582.3 13.1 %fusion.11 = f32[64,1,64]{2,1,0:T(1,128)S(1)} fusion(bf16[64,64,3584]{2,1,0:T(8,128)(2,1)} %bitcast.48, bf16[64,3584,1]{1,0,2:T(8,128)(2,1)S(1)} %bitcast.44), kind=kOutput, calls=%fused_computation.18 | convolution fusion | flops 29360128 | bytes 29835264 | tf_op jit(solution)/shard_map/mld,md->ml/dot_general | solution.py:76
  595.4 13.1 %fusion.13 = f32[64,1,64]{2,1,0:T(1,128)S(1)} fusion(bf16[64,64,3584]{2,1,0:T(8,128)(2,1)} %bitcast.49, bf16[64,3584,1]{1,0,2:T(8,128)(2,1)S(1)} %bitcast.43), kind=kOutput, calls=%fused_computation.20 | convolution fusion | flops 29360128 | bytes 29835264 | tf_op jit(solution)/shard_map/mld,md->ml/dot_general | solution.py:76
  608.4 29.4 %fusion.27 = f32[64,64,640]{2,1,0:T(8,128)} fusion(bf16[64,64,3584]{2,1,0:T(8,128)(2,1)} %bitcast.50, bf16[3584,640,1]{1,0,2:T(8,128)(2,1)} %bitcast.4), kind=kOutput, calls=%fused_computation.53 | convolution fusion | flops 18790481920 | bytes 44433408 | tf_op jit(solution)/shard_map/dot_general | solution.py:75
  637.8 5.0 all-to-all-done.1
  642.8 30.8 %multiply_convert_fusion = bf16[64,64,640]{2,1,0:T(8,128)(2,1)} fusion(f32[64,64,640]{2,1,0:T(8,128)} %fusion.27, f32[64,640]{1,0:T(8,128)S(1)} %fusion.24, f32[64,64]{1,0:T(8,128)S(1)} %get-tuple-element.9, f32[64,640]{1,0:T(8,128)S(1)} %fusion.23, f32[64,64]{1,0:T(8,128)S(1)} %get-tuple-element.10, bf16[64,64,3584]{2,1,0:T(8,128)(2,1)} %bitcast.51, ...), kind=kOutput, calls=%fused_computation.1 | convolution fusion | flops 18816696320 | bytes 50036736 | tf_op jit(solution)/shard_map/dot_general | solution.py:75
  673.6 4.8 all-to-all-start.2
  678.4 0.6 dynamic-slice
  679.7 0.2 dynamic-update-slice
  679.9 97.4 %all-reduce.4 = s32[64]{0:T(128)S(1)} all-reduce(s32[64]{0:T(128)S(1)} %dynamic-update-slice), channel_id=1, replica_groups=mesh['pop'=8,'tensor'=4] {'pop'}, use_global_device_ids=true, to_apply=%add.4 | all-reduce | flops 64 | bytes 512
  777.3 0.1 reduce-precision_convert_fusion
  777.5 4.7 fusion.7
  782.2 4.7 fusion.3
  786.9 3.3 copy.22
  790.3 2.6 slice.6
  (20 shorter events, 0.2 us)
Async XLA Ops:
  7.2 201.3 %reduce-scatter.2.cloned.1.call-start = ((), (), s32[]{:S(2)}) async-start(), calls=%async_computation.4 | async-start | bytes 8257536 | tf_op jit(solution)/shard_map/reduce_scatter | solution.py:54
  74.7 254.8 %all-gather.3.cloned.1.call-start = ((), (), s32[]{:S(2)}) async-start(), calls=%async_computation.5 | async-start | bytes 8257536 | tf_op jit(solution)/shard_map/all_gather | solution.py:63
  218.0 364.3 %all-gather.5.cloned.1.call-start = ((), (), s32[]{:S(2)}) async-start(), calls=%async_computation.6 | async-start | bytes 36700160 | tf_op jit(solution)/shard_map/all_gather | solution.py:64
  334.9 231.8 %all-to-all-start = ((bf16[448,8,640]{2,0,1:T(8,128)(2,1)}), bf16[448,8,640]{2,0,1:T(8,128)(2,1)}, u32[]{:S(2)}, u32[]{:S(2)}) async-start(bf16[448,8,640]{2,0,1:T(8,128)(2,1)} %bitcast.39), calls=%async_computation.1 | async-start | bytes 9175040 | tf_op jit(solution)/shard_map/all_to_all | solution.py:55
  339.7 7.2 copy-start
  343.7 119.0 %copy-start.1 = (bf16[8,4736]{1,0:T(8,128)(2,1)S(1)}, bf16[8,4736]{1,0:T(8,128)(2,1)}, u32[]{:S(2)}) copy-start(bf16[8,4736]{1,0:T(8,128)(2,1)} %param.19) | copy-start | bytes 227332
  343.7 150.8 %copy-start.2 = (bf16[8,3584]{1,0:T(8,128)(2,1)S(1)}, bf16[8,3584]{1,0:T(8,128)(2,1)}, u32[]{:S(2)}) copy-start(bf16[8,3584]{1,0:T(8,128)(2,1)} %param.16) | copy-start | bytes 172036
  343.7 182.1 %copy-start.3 = (bf16[8,3584]{1,0:T(8,128)(2,1)S(1)}, bf16[8,3584]{1,0:T(8,128)(2,1)}, u32[]{:S(2)}) copy-start(bf16[8,3584]{1,0:T(8,128)(2,1)} %param.17) | copy-start | bytes 172036
  566.7 76.1 %all-to-all-start.1 = ((bf16[448,8,640]{2,0,1:T(8,128)(2,1)}), bf16[448,8,640]{2,0,1:T(8,128)(2,1)}, u32[]{:S(2)}, u32[]{:S(2)}) async-start(bf16[448,8,640]{2,0,1:T(8,128)(2,1)} %bitcast.38), calls=%async_computation.2 | async-start | bytes 9175040 | tf_op jit(solution)/shard_map/all_to_all | solution.py:56
  673.6 4.8 copy-start.5
  673.6 6.1 copy-start.4
  673.6 113.3 %all-to-all-start.2 = ((bf16[8,512,640]{2,1,0:T(8,128)(2,1)}), bf16[8,512,640]{2,1,0:T(8,128)(2,1)}, u32[]{:S(2)}, u32[]{:S(2)}) async-start(bf16[8,512,640]{2,1,0:T(8,128)(2,1)} %bitcast.42), calls=%async_computation.3 | async-start | bytes 10485760 | tf_op jit(solution)/shard_map/all_to_all | solution.py:86
Sparse Core Ops, SparseCore 0:
  74.8 133.5 reduce-scatter.1
  218.1 111.3 all-gather.2
  331.1 175.9 all-gather.4
where the time goes:
time: 800 us; the launch traced here: 799 us
  blocking collectives  355 us (44%)
  waiting for transfers between devices  249 us (31%)
  matrix products  95.7 us (12%)
  local copies, waits for them, and re-layouts  47.3 us (6%)
  starting transfers between devices  25.3 us (3%)
  between operations  14.6 us (2%)
  other arithmetic  11.9 us (1%)
    reduce_scatter x1, waiting for transfers between devices, per_device(): lax.psum_scatter(partial_rows, 'pop', scatter_dimension=0, tiled=True)  133 us
    all_gather x1, blocking collectives, per_device(): lax.all_gather(gate_right, 'pop', axis=0, tiled=True)  116 us
    all_gather x1, waiting for transfers between devices, per_device(): some = lax.all_gather(own_normed, 'pop', axis=0, tiled=True)  111 us
    unnamed x1, blocking collectives  97.4 us
    dot_general x2, matrix products, project(): base = jnp.dot(normed, weight, preferred_element_type=jnp.float32)  60.2 us
    all_gather x1, blocking collectives, per_device(): lax.all_gather(up_left, 'pop', axis=0, tiled=True)  40.9 us
    all_gather x1, blocking collectives, per_device(): all_ids = lax.all_gather(token_ids, 'pop', axis=0, tiled=True)  32.3 us
    all_gather x1, blocking collectives, per_device(): lax.all_gather(up_right, 'pop', axis=0, tiled=True)  31.8 us
  transfers between devices with their start and end apart: 6, of which 3 were waited for; matrix products, arithmetic and copies ran while one was open for 10% of the time, Pallas kernels for 0%

commit v1 on v0

--- a/solution.py
+++ b/solution.py
@@ -45,7 +45,13 @@
     def pad_cols(x):
         return jnp.pad(x, ((0, 0), (0, padded - hidden_cols)))
 
-    all_ids = lax.all_gather(token_ids, "pop", axis=0, tiled=True)
+    size = lax.axis_size("pop")
+    current, pieces = (token_ids, [token_ids])
+    for _ in range(size - 1):
+        current = lax.ppermute(current, "pop", [(i, (i + 1) % size) for i in range(size)])
+        pieces.insert(0, current)
+    line = jnp.concatenate(pieces, axis=0)
+    all_ids = jnp.roll(line, (lax.axis_index("pop") + 1) * token_ids.shape[0], axis=0)
     all_ranks = lax.all_gather(ranks, "pop", axis=0, tiled=True)
     local_ids = all_ids.reshape(-1) - pop * table_rows
     owned = (local_ids >= 0) & (local_ids < table_rows)

time: 800 us -> 812 us (1.015)
  waiting for transfers between devices: 249 us -> 289 us
  blocking collectives: 355 us -> 323 us
    ppermute x0 -> x7, waiting for transfers between devices: none -> 42.6 us  [per_device(): lax.ppermute(current, 'pop', [(i, (i + 1) % size) for i in range(size)])]
    all_gather x1 -> x0, blocking collectives: 32.3 us -> none  [per_device(): all_ids = lax.all_gather(token_ids, 'pop', axis=0, tiled=True)]
  transfers between devices with their start and end apart: 6 -> 13, of which waited for: 3 -> 10; matrix products, arithmetic and copies ran while one was open for 10% -> 10% of each run, Pallas kernels for 0% -> 0%
where the time goes in v1:
time: 812 us; the launch traced here: 811 us
  blocking collectives  323 us (40%)
  waiting for transfers between devices  289 us (36%)
  matrix products  95.7 us (12%)
  local copies, waits for them, and re-layouts  48.7 us (6%)
  starting transfers between devices  28.3 us (3%)
  between operations  14.7 us (2%)
  other arithmetic  11.9 us (1%)
    reduce_scatter x1, waiting for transfers between devices, per_device(): lax.psum_scatter(partial_rows, 'pop', scatter_dimension=0, tiled=True)  129 us
    all_gather x1, blocking collectives, per_device(): lax.all_gather(gate_right, 'pop', axis=0, tiled=True)  116 us
    all_gather x1, waiting for transfers between devices, per_device(): some = lax.all_gather(own_normed, 'pop', axis=0, tiled=True)  111 us
    unnamed x1, blocking collectives  97.4 us
    dot_general x2, matrix products, project(): base = jnp.dot(normed, weight, preferred_element_type=jnp.float32)  60.1 us
    ppermute x7, waiting for transfers between devices, per_device(): lax.ppermute(current, 'pop', [(i, (i + 1) % size) for i in range(size)])  42.6 us
    all_gather x1, blocking collectives, per_device(): lax.all_gather(up_left, 'pop', axis=0, tiled=True)  40.9 us
    all_gather x1, blocking collectives, per_device(): lax.all_gather(up_right, 'pop', axis=0, tiled=True)  31.8 us
  transfers between devices with their start and end apart: 13, of which 10 were waited for; matrix products, arithmetic and copies ran while one was open for 10% of the time, Pallas kernels for 0%

profile of v1, /device:TPU:0, one launch (start us, length us, event | category | flops | bytes accessed | tf_op | source)
XLA Modules:
  0.0 810.7 jit_solution(15911301314163899613)
XLA Ops:
  7.2 0.0 reduce-scatter.2.cloned.1.call-start
  7.2 3.0 collective-permute-start
  10.2 4.8 collective-permute-done
  15.0 6.3 collective-permute-done.1
  21.3 6.3 collective-permute-done.2
  27.7 6.3 collective-permute-done.3
  34.0 6.3 collective-permute-done.4
  40.3 6.3 collective-permute-done.5
  46.6 6.3 collective-permute-done.6
  52.9 0.7 constant_dynamic-update-slice_fusion.8
  53.6 0.7 constant_dynamic-update-slice_fusion
  54.4 0.1 min.18
  54.5 0.1 min.16
  54.5 0.1 and.27
  54.7 27.8 %gather_fusion = bf16[4096,896]{1,0:T(8,128)(2,1)} fusion(bf16[9504,896]{1,0:T(8,128)(2,1)} %param.12, s32[4096]{0:T(1024)S(1)} %broadcast_clamp_fusion), kind=kCustom, calls=%fused_computation | custom fusion | bytes 14696448 | tf_op jit(solution)/shard_map/jit(_take)/gather | solution.py:58
  82.4 7.0 select_select_fusion
  89.5 0.0 all-gather.3.cloned.1.call-start
  89.6 0.8 dynamic-slice_convert_fusion
  90.3 129.5 %reduce-scatter.2.cloned.1.call-done = bf16[512,896]{1,0:T(8,128)(2,1)} async-done(((bf16[4096,896]{1,0:T(8,128)(2,1)}), bf16[512,896]{1,0:T(8,128)(2,1)}) %reduce-scatter.2.cloned.1.call-update) | async-done | bytes 917520 | tf_op jit(solution)/shard_map/reduce_scatter | solution.py:60
  219.8 1.4 fusion
  221.3 5.7 psum.7
  226.9 2.4 fusion.2
  229.3 0.0 all-gather.5.cloned.1.call-start
  229.4 111.5 %all-gather.3.cloned.1.call-done = bf16[4096,896]{1,0:T(8,128)(2,1)} async-done(((bf16[512,896]{1,0:T(8,128)(2,1)}), bf16[4096,896]{1,0:T(8,128)(2,1)}) %all-gather.3.cloned.1.call-update) | async-done | bytes 7340048 | tf_op jit(solution)/shard_map/all_gather | solution.py:69
  340.9 2.8 pad.14
  343.7 2.6 copy.30
  346.3 4.8 all-to-all-start
  351.1 4.0 pad.16
  355.1 3.2 copy.29
  358.3 115.7 %all_gather.24 = bf16[64,4736]{1,0:T(8,128)(2,1)S(1)} all-gather(bf16[8,4736]{1,0:T(8,128)(2,1)S(1)} %copy-done), channel_id=1, replica_groups=mesh['pop'=8,'tensor'=4] {'pop'}, dimensions={0}, use_global_device_ids=true | all-gather | bytes 681984 | tf_op jit(solution)/shard_map/all_gather | solution.py:74
  474.0 31.8 %all_gather.26 = bf16[64,4736]{1,0:T(8,128)(2,1)S(1)} all-gather(bf16[8,4736]{1,0:T(8,128)(2,1)S(1)} %copy-done.1), channel_id=1, replica_groups=mesh['pop'=8,'tensor'=4] {'pop'}, dimensions={0}, use_global_device_ids=true | all-gather | bytes 681984 | tf_op jit(solution)/shard_map/all_gather | solution.py:75
  505.9 31.3 %all_gather.23 = bf16[64,3584]{1,0:T(8,128)(2,1)S(1)} all-gather(bf16[8,3584]{1,0:T(8,128)(2,1)S(1)} %copy-done.2), channel_id=1, replica_groups=mesh['pop'=8,'tensor'=4] {'pop'}, dimensions={0}, use_global_device_ids=true | all-gather | bytes 516096 | tf_op jit(solution)/shard_map/all_gather | solution.py:72
  537.1 40.9 %all_gather.25 = bf16[64,3584]{1,0:T(8,128)(2,1)S(1)} all-gather(bf16[8,3584]{1,0:T(8,128)(2,1)S(1)} %copy-done.3), channel_id=1, replica_groups=mesh['pop'=8,'tensor'=4] {'pop'}, dimensions={0}, use_global_device_ids=true | all-gather | bytes 516096 | tf_op jit(solution)/shard_map/all_gather | solution.py:73
  578.0 15.6 %all-to-all-start.1 = ((bf16[448,8,640]{2,0,1:T(8,128)(2,1)}), bf16[448,8,640]{2,0,1:T(8,128)(2,1)}, u32[]{:S(2)}, u32[]{:S(2)}) async-start(bf16[448,8,640]{2,0,1:T(8,128)(2,1)} %bitcast.38), calls=%async_computation.2 | async-start | bytes 9175040 | tf_op jit(solution)/shard_map/all_to_all | solution.py:62
  593.7 13.1 %fusion.11 = f32[64,1,64]{2,1,0:T(1,128)S(1)} fusion(bf16[64,64,3584]{2,1,0:T(8,128)(2,1)} %bitcast.48, bf16[64,3584,1]{1,0,2:T(8,128)(2,1)S(1)} %bitcast.44), kind=kOutput, calls=%fused_computation.18 | convolution fusion | flops 29360128 | bytes 29835264 | tf_op jit(solution)/shard_map/mld,md->ml/dot_general | solution.py:82
  606.7 13.1 %fusion.13 = f32[64,1,64]{2,1,0:T(1,128)S(1)} fusion(bf16[64,64,3584]{2,1,0:T(8,128)(2,1)} %bitcast.49, bf16[64,3584,1]{1,0,2:T(8,128)(2,1)S(1)} %bitcast.43), kind=kOutput, calls=%fused_computation.20 | convolution fusion | flops 29360128 | bytes 29835264 | tf_op jit(solution)/shard_map/mld,md->ml/dot_general | solution.py:82
  619.8 29.4 %fusion.28 = f32[64,64,640]{2,1,0:T(8,128)} fusion(bf16[64,64,3584]{2,1,0:T(8,128)(2,1)} %bitcast.50, bf16[3584,640,1]{1,0,2:T(8,128)(2,1)} %bitcast.4), kind=kOutput, calls=%fused_computation.70 | convolution fusion | flops 18790481920 | bytes 44433408 | tf_op jit(solution)/shard_map/dot_general | solution.py:81
  649.1 5.0 all-to-all-done.1
  654.1 30.8 %multiply_convert_fusion = bf16[64,64,640]{2,1,0:T(8,128)(2,1)} fusion(f32[64,64,640]{2,1,0:T(8,128)} %fusion.28, f32[64,640]{1,0:T(8,128)S(1)} %fusion.24, f32[64,64]{1,0:T(8,128)S(1)} %get-tuple-element.9, f32[64,640]{1,0:T(8,128)S(1)} %fusion.23, f32[64,64]{1,0:T(8,128)S(1)} %get-tuple-element.10, bf16[64,64,3584]{2,1,0:T(8,128)(2,1)} %bitcast.51, ...), kind=kOutput, calls=%fused_computation.1 | convolution fusion | flops 18816696320 | bytes 50036736 | tf_op jit(solution)/shard_map/dot_general | solution.py:81
  684.9 4.8 all-to-all-start.2
  689.7 0.6 dynamic-slice
  691.0 0.2 dynamic-update-slice
  691.2 97.4 %all-reduce.4 = s32[64]{0:T(128)S(1)} all-reduce(s32[64]{0:T(128)S(1)} %dynamic-update-slice), channel_id=1, replica_groups=mesh['pop'=8,'tensor'=4] {'pop'}, use_global_device_ids=true, to_apply=%add.4 | all-reduce | flops 64 | bytes 512
  788.7 0.1 reduce-precision_convert_fusion
  788.8 4.7 fusion.7
  793.5 4.7 fusion.3
  798.3 3.3 copy.22
  801.6 2.6 slice.6
  (49 shorter events, 0.3 us)
Async XLA Ops:
  7.2 212.7 %reduce-scatter.2.cloned.1.call-start = ((), (), s32[]{:S(2)}) async-start(), calls=%async_computation.4 | async-start | bytes 8257536 | tf_op jit(solution)/shard_map/reduce_scatter | solution.py:60
  7.2 7.8 collective-permute-start
  15.0 6.3 collective-permute-start.1
  21.3 6.3 collective-permute-start.2
  27.6 6.3 collective-permute-start.3
  34.0 6.3 collective-permute-start.4
  40.3 6.3 collective-permute-start.5
  46.6 6.3 collective-permute-start.6
  89.5 251.3 %all-gather.3.cloned.1.call-start = ((), (), s32[]{:S(2)}) async-start(), calls=%async_computation.5 | async-start | bytes 8257536 | tf_op jit(solution)/shard_map/all_gather | solution.py:69
  229.3 364.3 %all-gather.5.cloned.1.call-start = ((), (), s32[]{:S(2)}) async-start(), calls=%async_computation.6 | async-start | bytes 36700160 | tf_op jit(solution)/shard_map/all_gather | solution.py:70
  346.3 231.8 %all-to-all-start = ((bf16[448,8,640]{2,0,1:T(8,128)(2,1)}), bf16[448,8,640]{2,0,1:T(8,128)(2,1)}, u32[]{:S(2)}, u32[]{:S(2)}) async-start(bf16[448,8,640]{2,0,1:T(8,128)(2,1)} %bitcast.39), calls=%async_computation.1 | async-start | bytes 9175040 | tf_op jit(solution)/shard_map/all_to_all | solution.py:61
  351.1 7.2 copy-start
  355.0 119.0 %copy-start.1 = (bf16[8,4736]{1,0:T(8,128)(2,1)S(1)}, bf16[8,4736]{1,0:T(8,128)(2,1)}, u32[]{:S(2)}) copy-start(bf16[8,4736]{1,0:T(8,128)(2,1)} %param.19) | copy-start | bytes 227332
  355.1 150.8 %copy-start.2 = (bf16[8,3584]{1,0:T(8,128)(2,1)S(1)}, bf16[8,3584]{1,0:T(8,128)(2,1)}, u32[]{:S(2)}) copy-start(bf16[8,3584]{1,0:T(8,128)(2,1)} %param.16) | copy-start | bytes 172036
  355.1 182.1 %copy-start.3 = (bf16[8,3584]{1,0:T(8,128)(2,1)S(1)}, bf16[8,3584]{1,0:T(8,128)(2,1)}, u32[]{:S(2)}) copy-start(bf16[8,3584]{1,0:T(8,128)(2,1)} %param.17) | copy-start | bytes 172036
  578.0 76.1 %all-to-all-start.1 = ((bf16[448,8,640]{2,0,1:T(8,128)(2,1)}), bf16[448,8,640]{2,0,1:T(8,128)(2,1)}, u32[]{:S(2)}, u32[]{:S(2)}) async-start(bf16[448,8,640]{2,0,1:T(8,128)(2,1)} %bitcast.38), calls=%async_computation.2 | async-start | bytes 9175040 | tf_op jit(solution)/shard_map/all_to_all | solution.py:62
  684.9 4.8 copy-start.5
  684.9 6.1 copy-start.4
  684.9 113.3 %all-to-all-start.2 = ((bf16[8,512,640]{2,1,0:T(8,128)(2,1)}), bf16[8,512,640]{2,1,0:T(8,128)(2,1)}, u32[]{:S(2)}, u32[]{:S(2)}) async-start(bf16[8,512,640]{2,1,0:T(8,128)(2,1)} %bitcast.42), calls=%async_computation.3 | async-start | bytes 10485760 | tf_op jit(solution)/shard_map/all_to_all | solution.py:92
Sparse Core Ops, SparseCore 0:
  89.6 130.1 reduce-scatter.1
  229.5 111.3 all-gather.2
  342.4 175.9 all-gather.4
